TPU v7x, 32 devices: a whole 2x2x4 slice. The times are simulated.
32 devices in a mesh: tile: 8 (over y, x, core), head: 4 (over z).
Axes of the slice: x: 2, y: 2, z: 4, core: 2. Of those that a mesh axis runs over, the one named last changes fastest.
Arguments:
- self_query: bfloat16 [1024, 5120], P('tile', 'head')
- self_key: bfloat16 [1024, 5120], P('tile', 'head')
- self_value: bfloat16 [1024, 5120], P('tile', 'head'), may hold values from -6 to 6
- cross_query: bfloat16 [1024, 5120], P('tile', 'head')
- text_key: bfloat16 [2048, 5120], P('tile', 'head'), as said below
- text_value: bfloat16 [2048, 5120], P('tile', 'head'), as said below
- query_gain: float32 [5120], P('head'), may hold values from 0.5 to 1.5
- key_gain: float32 [5120], P('head'), may hold values from 0.5 to 1.5
- cross_gain: float32 [5120], P('head'), may hold values from 0.5 to 1.5
- text_gain: float32 [5120], P('head'), may hold values from 0.5 to 1.5
- tile_item: int32 [8], replicated, may hold values from 0 to 3, as said below
- row_count: int32 [8], replicated, may hold values from 32 to 128, as said below
- text_len: int32 [8], replicated, may hold values from 2 to 256, as said below
Outputs:
- attended: bfloat16 [1024, 5120], P('tile', 'head')
Inputs may be any that keep to these rules, and one draw needn't show every extreme that they name: `tile_item`: never falling and 0 on the first tile; every item holds 1 to 4 consecutive tiles, some item holds exactly 4, and there are 4 items. `row_count`: some tile holds exactly 128. `text_len`: entries past the last item are not used; some item has exactly 256. `text_key`: tiles of one item hold the same text rows. `text_value`: tiles of one item hold the same text rows.
All inputs are finite; a program needn't handle non-finite values.
Results may differ from a plain program's by a relative error of at most 0.0015.
The roundings to bfloat16 on the way count: a program that leaves them out, or rounds other values in their place, can miss the bound.
Values may be sent and summed in bfloat16 or wider, within the bound.
A program may use at most 64 MiB of HBM per device.

v0:
```python
import functools
import math

import jax
import jax.numpy as jnp
import numpy as np
from jax import lax
from jax.experimental import pallas as pl
from jax.experimental.pallas import tpu as pltpu
from jax.sharding import PartitionSpec as P

D = 5120
HD = 128
HGT = 30
WID = 52


EPSILON = 1e-06


def shifted(value, axis, by):
    peers = lax.axis_size(axis)
    pairs = [(i, i + by) for i in range(peers) if 0 <= i + by < peers]
    return lax.ppermute(value, axis, pairs)


def frequencies(amount, dimension):
    return 1.0 / 10000.0 ** (jnp.arange(amount, dtype=jnp.float32) * 2.0 / dimension)


def rope_angles(positions):
    spatial = HD // 6
    temporal = HD // 2 - 2 * spatial
    frame = (positions // (HGT * WID)).astype(jnp.float32)
    height = (positions // WID % HGT).astype(jnp.float32)
    across = (positions % WID).astype(jnp.float32)
    return jnp.concatenate(
        [
            frame[:, None] * frequencies(temporal, 2 * temporal)[None, :],
            height[:, None] * frequencies(spatial, 2 * spatial)[None, :],
            across[:, None] * frequencies(spatial, 2 * spatial)[None, :],
        ],
        axis=1,
    )


def pair_partner(matrix):
    index = jnp.arange(matrix.shape[-1])
    return jnp.where(index % 2 == 0, -jnp.roll(matrix, -1, axis=-1), jnp.roll(matrix, 1, axis=-1))


def rotate(matrix, angle):
    cosine = jnp.repeat(jnp.cos(angle), 2, axis=1)
    sine = jnp.repeat(jnp.sin(angle), 2, axis=1)
    shaped = matrix.reshape(matrix.shape[0], matrix.shape[1] // HD, HD)
    turned = shaped * cosine[:, None, :] + pair_partner(shaped) * sine[:, None, :]
    return turned.reshape(matrix.shape)


def scaled_rows(values, mean_square, gain):
    return values * lax.rsqrt(mean_square[:, None] + EPSILON) * gain[None, :]


def attend_head(query, key_rows, value_rows, live):
    scale = 1.0 / math.sqrt(HD)
    scores = (
        lax.dot_general(
            query, key_rows, (((1,), (1,)), ((), ())), preferred_element_type=jnp.float32
        )
        * scale
    )
    scores = jnp.where(live[None, :], scores, -1e30)
    highest = jnp.max(scores, axis=1, keepdims=True)
    weights = jnp.exp(scores - highest)
    total = jnp.sum(weights, axis=1, keepdims=True)
    mixed = jnp.dot(weights.astype(jnp.bfloat16), value_rows, preferred_element_type=jnp.float32)
    return mixed / total


def per_device(
    self_query,
    self_key,
    self_value,
    cross_query,
    text_key,
    text_value,
    query_gain,
    key_gain,
    cross_gain,
    text_gain,
    tile_item,
    row_count,
    text_len,
):
    row_total = self_query.shape[0]
    text_total = text_key.shape[0]
    head_total = self_query.shape[1] // HD
    tile_here = lax.axis_index("tile")
    tile_total = lax.axis_size("tile")
    span = min(7, tile_total // 2)
    item_here = tile_item[tile_here]
    first_tile = jnp.sum((tile_item < item_here).astype(jnp.int32))
    positions = (tile_here - first_tile) * row_total + jnp.arange(row_total, dtype=jnp.int32)
    angle = rope_angles(positions)
    query_float = self_query.astype(jnp.float32)
    key_float = self_key.astype(jnp.float32)
    cross_float = cross_query.astype(jnp.float32)
    text_float = text_key.astype(jnp.float32)
    query_sq, key_sq, cross_sq, text_sq = lax.psum(
        (
            jnp.sum(query_float * query_float, axis=1),
            jnp.sum(key_float * key_float, axis=1),
            jnp.sum(cross_float * cross_float, axis=1),
            jnp.sum(text_float * text_float, axis=1),
        ),
        "head",
    )
    queries = rotate(scaled_rows(query_float, query_sq / D, query_gain), angle).astype(jnp.bfloat16)
    rotated_keys = rotate(scaled_rows(key_float, key_sq / D, key_gain), angle).astype(jnp.bfloat16)
    cross = scaled_rows(cross_float, cross_sq / D, cross_gain).astype(jnp.bfloat16)
    texts = scaled_rows(text_float, text_sq / D, text_gain).astype(jnp.bfloat16)

    def live_rows(source):
        inside = (source >= 0) & (source < tile_total)
        clipped = jnp.clip(source, 0, tile_total - 1)
        same_item = inside & (tile_item[clipped] == item_here)
        return same_item & (jnp.arange(row_total, dtype=jnp.int32) < row_count[clipped])

    key_parts = [rotated_keys]
    value_parts = [self_value]
    live_parts = [live_rows(tile_here)]
    for distance in range(1, span):
        for offset in (distance, -distance):
            moved_keys, moved_values = shifted((rotated_keys, self_value), "tile", offset)
            key_parts.append(moved_keys)
            value_parts.append(moved_values)
            live_parts.append(live_rows(tile_here - offset))
    keys_all = jnp.concatenate(key_parts, axis=0)
    values_all = jnp.concatenate(value_parts, axis=0)
    live_all = jnp.concatenate(live_parts, axis=0)
    text_live = jnp.arange(text_total, dtype=jnp.int32) < text_len[item_here]

    def per_head(head_index):
        first_column = head_index * HD

        def columns(matrix):
            return lax.dynamic_slice_in_dim(matrix, first_column, HD, 1)

        local_part = attend_head(columns(queries), columns(keys_all), columns(values_all), live_all)
        text_part = attend_head(columns(cross), columns(texts), columns(text_value), text_live)
        return (local_part + text_part).astype(jnp.bfloat16)

    head_outputs = lax.map(per_head, jnp.arange(head_total, dtype=jnp.int32))
    return jnp.moveaxis(head_outputs, 0, 1).reshape(row_total, head_total * HD)


TILES = 8
SHARDS = 4
SPAN = 4
WIDE = 256
BIG = -1e30


def needs(start):
    found = []
    for t in range(TILES):
        if start <= t < start + SPAN:
            found.append({b for b in range(start, start + SPAN) if b != t})
        else:
            near = {t - 1, t + 1} & set(range(TILES))
            found.append({b for b in near if not start <= b < start + SPAN})
    return found


def window(start):
    return [start if start <= t < start + SPAN else (0 if t < start else TILES - SPAN) for t in range(TILES)]


def chip_edges(start, block, chips, far):
    if start > 2:
        return [(3 - a, 3 - c) for a, c in chip_edges(TILES - SPAN - start, TILES - 1 - block, {3 - c for c in chips}, far)]
    home = block // 2
    if start == 0 and block < SPAN and far:
        return [(0, 2), (2, 3), (3, 1)] if home == 0 else [(1, 3), (3, 2), (2, 0)]
    if start == 1 and block in (2, 3, 4):
        return {2: [(1, 0), (0, 2)], 3: [(1, 0), (1, 3), (3, 2)], 4: [(2, 0), (2, 3), (3, 1)]}[block]
    if start == 2 and 2 <= block <= 5:
        return {2: [(1, 0), (0, 2)], 3: [(1, 3), (3, 2)], 4: [(2, 3), (3, 1)], 5: [(2, 0), (0, 1)]}[block]
    return [(home, chip) for chip in sorted(chips)]


def edges_of(start, far):
    need = needs(start)
    edges = []
    for b in range(TILES):
        users = [t for t in range(TILES) if b in need[t]]
        home, core = b // 2, b % 2
        held = {home: (b, 0)}
        if b ^ 1 in users:
            edges.append((b, b ^ 1, b, 0))
        chips = {t // 2 for t in users} - {home}
        for a, c in chip_edges(start, b, chips, far):
            src, depth = held[a]
            same = 2 * c + core
            onward = any(x == c for x, _ in chip_edges(start, b, chips, far))
            entry = same if same in users or onward or same ^ 1 not in users else same ^ 1
            edges.append((src, entry, b, depth))
            held[c] = (entry, depth + 1)
            if entry ^ 1 in users:
                edges.append((entry, entry ^ 1, b, depth + 1))
    return edges


def plan_of(start, far):
    edges = edges_of(start, far)
    first = [[e[1] for e in sorted(edges) if e[3] == 0 and e[0] == t] for t in range(TILES)]
    first = [sorted(f, key=lambda v, t=t: v == t ^ 1) for t, f in enumerate(first)]
    rounds = []
    for depth in range(1, 1 + max([e[3] for e in edges])):
        events = []
        for t in range(TILES):
            mine = sorted({e[2] for e in edges if e[3] == depth and e[0] == t})
            dests = [(b, sorted([e[1] for e in edges if e[0] == t and e[2] == b], key=lambda v: v == t ^ 1)) for b in mine]
            events.append(dests)
        for k in range(max(len(e) for e in events)):
            rounds.append([e[k] if k < len(e) else None for e in events])
    gets = [{e[2] for e in edges if e[1] == t} for t in range(TILES)]
    passed = [{e[2] for e in edges if e[3] > 0 and e[0] == t} for t in range(TILES)]
    return first, rounds, gets, passed


def kernel(
    start,
    q_in, k_in, v_in, c_in, tk_in, tv_in,
    q_gain_in, k_gain_in, c_gain_in, t_gain_in,
    cos_in, sin_in, item_in, count_in, len_in,
    out_ref,
    q_gain, k_gain, c_gain, t_gain,
    cos_ref, sin_ref, tile_item, row_count, text_len,
    q_raw, k_raw, c_raw, t_raw, t_val,
    queries, cross, texts, text_out,
    kbuf, vbuf, sums, live, text_live,
    in_sem, y_send, y_recv, z_send, z_recv, send_sem, recv_sem,
):
    me = lax.axis_index("tile")
    shard = lax.axis_index("head")
    rows = q_in.shape[0]
    heads = q_in.shape[1] // HD
    groups = q_in.shape[1] // WIDE
    per = WIDE // HD
    txt = tk_in.shape[0]

    def pick(values):
        result = jnp.int32(values[0])
        for i in range(1, TILES):
            if values[i] != values[0]:
                result = jnp.where(me == i, jnp.int32(values[i]), result)
        return result

    loads = [
        pltpu.make_async_copy(src, dst, in_sem.at[i])
        for i, (src, dst) in enumerate(
            ((k_in, k_raw), (q_in, q_raw), (c_in, c_raw), (tk_in, t_raw), (tv_in, t_val),
             (item_in, tile_item), (count_in, row_count), (len_in, text_len), (cos_in, cos_ref), (sin_in, sin_ref),
             (k_gain_in, k_gain), (q_gain_in, q_gain), (c_gain_in, c_gain), (t_gain_in, t_gain))
        )
    ]
    own = [
        pltpu.make_async_copy(v_in.at[:, g * WIDE : (g + 1) * WIDE], vbuf.at[me, g], in_sem.at[len(loads) + g])
        for g in range(groups)
    ]
    for load in own + loads:
        load.start()

    barrier = pltpu.get_barrier_semaphore()
    for o in range(1, TILES):
        pl.semaphore_signal(barrier, inc=1, device_id=(lax.rem(me + o, TILES), shard), device_id_type=pl.DeviceIdType.MESH)
    for o in range(1, SHARDS):
        pl.semaphore_signal(barrier, inc=1, device_id=(me, lax.rem(shard + o, SHARDS)), device_id_type=pl.DeviceIdType.MESH)
    pl.semaphore_wait(barrier, TILES + SHARDS - 2)

    near, far = plan_of(start, False), plan_of(start, True)
    split = start in (0, TILES - SPAN)
    order = ([groups - 1] if split else []) + list(range(groups - 1 if split else groups))
    base = pick(window(start))

    def plan(g):
        return far if split and g == groups - 1 else near

    def send(src, buf, kind, block, g, lane, dest):
        return pltpu.make_async_remote_copy(
            src_ref=src,
            dst_ref=buf.at[block, g],
            send_sem=send_sem.at[kind, block, g, lane],
            recv_sem=recv_sem.at[kind, block, g],
            device_id=(dest, shard),
            device_id_type=pl.DeviceIdType.MESH,
        )

    def each_first(first, act):
        for lane in range(max(len(f) for f in first)):
            dests = [f[lane] if lane < len(f) else -1 for f in first]
            dest = pick(dests)

            def run(lane=lane, dest=dest):
                act(lane, dest)

            if -1 in dests:
                pl.when(dest >= 0)(run)
            else:
                run()

    def each_round(rounds, act):
        for one in rounds:
            block = pick([e[0] if e else -1 for e in one])
            widest = max(len(e[1]) for e in one if e)
            dests = [pick([e[1][i] if e and i < len(e[1]) else -1 for e in one]) for i in range(widest)]

            def run(block=block, dests=dests):
                act(block, dests)

            if any(e is None for e in one):
                pl.when(block >= 0)(run)
            else:
                run()

    def pass_on(rounds, buf, kind, g):
        def act(block, dests):
            send(buf.at[block, g], buf, kind, block, g, 0, me).wait_recv()
            for lane, dest in enumerate(dests):

                def go(lane=lane, dest=dest):
                    send(buf.at[block, g], buf, kind, block, g, lane, dest).start()

                pl.when(dest >= 0)(go)

        each_round(rounds, act)

    def arrive(which, buf, kind, g):
        _, _, gets, passed = which
        for j in range(SPAN):
            waits = [int(window(start)[t] + j in gets[t] and window(start)[t] + j not in passed[t]) for t in range(TILES)]

            def go(j=j):
                send(buf.at[base + j, g], buf, kind, base + j, g, 0, me).wait_recv()

            if any(waits):
                pl.when(pick(waits) == 1)(go)

    def drain(which, buf, kind, g):
        def of_first(lane, dest):
            send(buf.at[me, g], buf, kind, me, g, lane, dest).wait_send()

        each_first(which[0], of_first)

        def of_round(block, dests):
            for lane, dest in enumerate(dests):

                def go(lane=lane, dest=dest):
                    send(buf.at[block, g], buf, kind, block, g, lane, dest).wait_send()

                pl.when(dest >= 0)(go)

        each_round(which[1], of_round)

    for g in order:
        own[g].wait()

        def of_value(lane, dest, g=g):
            send(vbuf.at[me, g], vbuf, 0, me, g, lane, dest).start()

        each_first(plan(g)[0], of_value)

    for which, g0, g1 in ((near, 0, groups - 1 if split else groups), (far, groups - 1, groups)):
        if g1 == groups and which is far and not split:
            continue
        for j in range(SPAN):
            empty = [int(window(start)[t] + j not in which[2][t] and window(start)[t] + j != t) for t in range(TILES)]
            if any(empty):

                @pl.when(pick(empty) == 1)
                def _(j=j, g0=g0, g1=g1):
                    for g in range(g0, g1):
                        vbuf[base + j, g] = jnp.zeros((rows, WIDE), jnp.bfloat16)

    def partial(ref, r0):
        total = jnp.zeros((rows, HD), jnp.float32)
        for i in range(heads):
            part = ref[r0 : r0 + rows, i * HD : (i + 1) * HD].astype(jnp.float32)
            total = total + part * part
        column = jnp.sum(total, axis=1, keepdims=True)
        return jnp.broadcast_to(column, (rows, HD)).T[0:8, :]

    def share(o, slot, first):
        span = pl.ds(0, rows) if first else pl.ds(rows, 2 * rows + txt)
        return pltpu.make_async_remote_copy(
            src_ref=sums.at[slot, :, span],
            dst_ref=sums.at[slot, :, span],
            send_sem=(y_send if first else z_send).at[o - 1],
            recv_sem=(y_recv if first else z_recv).at[slot],
            device_id=(me, lax.rem(shard + o, SHARDS)),
            device_id_type=pl.DeviceIdType.MESH,
        )

    def gather(first):
        for o in range(1, SHARDS):
            share(o, lax.rem(shard + o, SHARDS), first).wait_recv()

    pieces = [(k_raw, 0), (q_raw, 0), (c_raw, 0)] + [(t_raw, r) for r in range(0, txt, rows)]
    for i, (ref, r0) in enumerate(pieces):
        if i < 4:
            loads[i].wait()
        sums[shard, :, i * rows : (i + 1) * rows] = partial(ref, r0)
        if i in (0, len(pieces) - 1):
            for o in range(1, SHARDS):
                share(o, shard, i == 0).start()

    for load in loads[5:]:
        load.wait()
    item = tile_item[me]
    before = jnp.int32(0)
    for t in range(TILES):
        before = before + jnp.where(tile_item[t] < item, 1, 0).astype(jnp.int32)
    place = me - before
    words = jnp.int32(0)
    for t in range(TILES):
        words = words + jnp.where(item == t, text_len[t], 0).astype(jnp.int32)
    lane_row = lax.broadcasted_iota(jnp.int32, (8, rows), 1)
    for j in range(SPAN):
        block = base + j
        limit = jnp.where(tile_item[block] == item, row_count[block], 0)
        live[:, j * rows : (j + 1) * rows] = jnp.where(lane_row < limit, 0.0, 1.0).astype(jnp.float32)
    lane_text = lax.broadcasted_iota(jnp.int32, (8, txt), 1)
    text_live[...] = jnp.where(lane_text < words, 0.0, 1.0).astype(jnp.float32)

    gather(True)

    def scale_of(i):
        span = slice(i * rows, (i + 1) * rows)
        total = (sums[0, :, span] + sums[1, :, span]) + (sums[2, :, span] + sums[3, :, span])
        scale = lax.rsqrt(total / D + EPSILON)
        return jnp.broadcast_to(scale[0:1, :], (HD, rows)).T

    cosine = cos_ref[0:rows, :]
    sine = sin_ref[0:rows, :]
    for j in range(1, SPAN):
        cosine = jnp.where(place == j, cos_ref[j * rows : (j + 1) * rows, :], cosine)
        sine = jnp.where(place == j, sin_ref[j * rows : (j + 1) * rows, :], sine)
    even = lax.broadcasted_iota(jnp.int32, (rows, HD), 1) % 2 == 0

    def turned(values):
        partner = jnp.where(even, pltpu.roll(values, HD - 1, 1), pltpu.roll(values, 1, 1))
        return values * cosine + partner * sine

    k_scale = scale_of(0)
    for g in order:
        for i in range(per):
            cols = slice(g * WIDE + i * HD, g * WIDE + (i + 1) * HD)
            scaled = k_raw[:, cols].astype(jnp.float32) * k_scale * k_gain[cols][None, :]
            kbuf[me, g, :, i * HD : (i + 1) * HD] = turned(scaled).astype(jnp.bfloat16)

        def of_key(lane, dest, g=g):
            send(kbuf.at[me, g], kbuf, 1, me, g, lane, dest).start()

        each_first(plan(g)[0], of_key)

    due = [(groups - 1, far[1][:2])] if split else []
    due += [(g, near[1]) for g in range(groups - 1 if split else groups)]
    due += [(groups - 1, far[1][2:])] if split else []

    def pass_values(count):
        for g, rounds in due[:count]:
            pass_on(rounds, vbuf, 0, g)
        del due[:count]

    pass_values(1)
    gather(False)
    q_scale = scale_of(1)
    for i in range(heads):
        cols = slice(i * HD, (i + 1) * HD)
        scaled = q_raw[:, cols].astype(jnp.float32) * q_scale * q_gain[cols][None, :]
        queries[i // per, :, (i % per) * HD : (i % per + 1) * HD] = turned(scaled).astype(jnp.bfloat16)
    c_scale = scale_of(2)
    for i in range(heads):
        cols = slice(i * HD, (i + 1) * HD)
        cross[i // per, :, (i % per) * HD : (i % per + 1) * HD] = (
            c_raw[:, cols].astype(jnp.float32) * c_scale * c_gain[cols][None, :]
        ).astype(jnp.bfloat16)
    for r in range(txt // rows):
        t_scale = scale_of(3 + r)
        span = slice(r * rows, (r + 1) * rows)
        for i in range(heads):
            cols = slice(i * HD, (i + 1) * HD)
            texts[i // per, span, (i % per) * HD : (i % per + 1) * HD] = (
                t_raw[span, cols].astype(jnp.float32) * t_scale * t_gain[cols][None, :]
            ).astype(jnp.bfloat16)

    scale = 1.0 / math.sqrt(HD)

    def weigh(scores, dead):
        scores = jnp.where(dead > 0.5, BIG, scores * scale)
        highest = jnp.max(scores, axis=1, keepdims=True)
        weights = jnp.exp(scores - highest)
        total = jnp.sum(weights, axis=1, keepdims=True)
        return weights.astype(jnp.bfloat16), total

    def against(query, key):
        return lax.dot_general(query, key, (((1,), (1,)), ((), ())), preferred_element_type=jnp.float32)

    loads[4].wait()

    pass_values(1)
    dead_text = text_live[0:1, :]
    for i in range(heads):
        g, cols = i // per, slice((i % per) * HD, (i % per + 1) * HD)
        weights, total = weigh(against(cross[g, :, cols], texts[g, :, cols]), dead_text)
        mixed = jnp.dot(weights, t_val[:, i * HD : (i + 1) * HD], preferred_element_type=jnp.float32)
        text_out[g, :, cols] = mixed / total
        if i == heads // 2 - 1:
            pass_values(2)
    pass_values(len(due))
    if split:
        pass_on(far[1][:2], kbuf, 1, groups - 1)

    def self_group(which, rounds, g):
        pass_on(rounds, kbuf, 1, g)
        arrive(which, vbuf, 0, g)
        arrive(which, kbuf, 1, g)
        dead = live[0:1, :]
        for i in range(per):
            cols = slice(i * HD, (i + 1) * HD)
            query = queries[g, :, cols]
            scores = jnp.concatenate([against(query, kbuf[base + j, g, :, cols]) for j in range(SPAN)], axis=1)
            weights, total = weigh(scores, dead)
            mixed = jnp.zeros((rows, HD), jnp.float32)
            for j in range(SPAN):
                mixed = mixed + jnp.dot(
                    weights[:, j * rows : (j + 1) * rows], vbuf[base + j, g, :, cols], preferred_element_type=jnp.float32
                )
            at = pl.ds(pl.multiple_of(g * WIDE + i * HD, HD), HD)
            out_ref[:, at] = (mixed / total + text_out[g, :, cols]).astype(jnp.bfloat16)

    def near_group(g, carry):
        self_group(near, near[1], g)
        return carry

    def near_drain(g, carry):
        drain(near, vbuf, 0, g)
        drain(near, kbuf, 1, g)
        return carry

    lax.fori_loop(0, groups - 1 if split else groups, near_group, 0)
    if split:
        self_group(far, far[1][2:], groups - 1)
        drain(far, vbuf, 0, groups - 1)
        drain(far, kbuf, 1, groups - 1)
    lax.fori_loop(0, groups - 1 if split else groups, near_drain, 0)
    for first in (True, False):
        for o in range(1, SHARDS):
            share(o, shard, first).wait_send()


def rotary_tables(rows):
    positions = np.arange(SPAN * rows)
    spatial = HD // 6
    temporal = HD // 2 - 2 * spatial

    def rates(amount):
        return (1.0 / 10000.0 ** (np.arange(amount) / amount)).astype(np.float32)

    angle = np.concatenate(
        [
            (positions // (HGT * WID)).astype(np.float32)[:, None] * rates(temporal)[None, :],
            (positions // WID % HGT).astype(np.float32)[:, None] * rates(spatial)[None, :],
            (positions % WID).astype(np.float32)[:, None] * rates(spatial)[None, :],
        ],
        axis=1,
    ).astype(np.float64)
    cosine = np.repeat(np.cos(angle), 2, axis=1).astype(np.float32)
    sine = np.repeat(np.sin(angle), 2, axis=1).astype(np.float32)
    sine[:, 0::2] *= -1.0
    return cosine, sine


def fused(
    self_query, self_key, self_value, cross_query, text_key, text_value,
    query_gain, key_gain, cross_gain, text_gain, tile_item, row_count, text_len,
):
    rows, width = self_query.shape
    txt = text_key.shape[0]
    groups = width // WIDE
    cosine, sine = rotary_tables(rows)
    bf16, f32 = jnp.bfloat16, jnp.float32
    hbm = pl.BlockSpec(memory_space=pl.ANY)
    vmem = pl.BlockSpec(memory_space=pltpu.VMEM)

    def call(start):
        return pl.pallas_call(
            functools.partial(kernel, start),
            out_shape=jax.ShapeDtypeStruct((rows, width), bf16),
            in_specs=[hbm] * 15,
            out_specs=vmem,
            scratch_shapes=[pltpu.VMEM((width,), f32)] * 4
            + [pltpu.VMEM((SPAN * rows, HD), f32)] * 2
            + [pltpu.SMEM((TILES,), jnp.int32)] * 3
            + [
                pltpu.VMEM((rows, width), bf16),
                pltpu.VMEM((rows, width), bf16),
                pltpu.VMEM((rows, width), bf16),
                pltpu.VMEM((txt, width), bf16),
                pltpu.VMEM((txt, width), bf16),
                pltpu.VMEM((groups, rows, WIDE), bf16),
                pltpu.VMEM((groups, rows, WIDE), bf16),
                pltpu.VMEM((groups, txt, WIDE), bf16),
                pltpu.VMEM((groups, rows, WIDE), f32),
                pltpu.VMEM((TILES, groups, rows, WIDE), bf16),
                pltpu.VMEM((TILES, groups, rows, WIDE), bf16),
                pltpu.VMEM((SHARDS, 8, 3 * rows + txt), f32),
                pltpu.VMEM((8, SPAN * rows), f32),
                pltpu.VMEM((8, txt), f32),
                pltpu.SemaphoreType.DMA((14 + groups,)),
                pltpu.SemaphoreType.DMA((SHARDS - 1,)),
                pltpu.SemaphoreType.DMA((SHARDS,)),
                pltpu.SemaphoreType.DMA((SHARDS - 1,)),
                pltpu.SemaphoreType.DMA((SHARDS,)),
                pltpu.SemaphoreType.DMA((2, TILES, groups, 4)),
                pltpu.SemaphoreType.DMA((2, TILES, groups)),
            ],
            compiler_params=pltpu.CompilerParams(
                collective_id=start, has_side_effects=True, vmem_limit_bytes=40 * 1024 * 1024
            ),
        )

    operands = (
        self_query, self_key, self_value, cross_query, text_key, text_value,
        query_gain, key_gain, cross_gain, text_gain,
        jnp.asarray(cosine), jnp.asarray(sine), tile_item, row_count, text_len,
    )
    full = tile_item[SPAN - 1 :] == tile_item[: TILES - SPAN + 1]
    start = jnp.argmax(full).astype(jnp.int32)
    return lax.switch(start, [call(s) for s in range(TILES - SPAN + 1)], *operands)


def solution(mesh):
    in_specs = (
        P("tile", "head"),
        P("tile", "head"),
        P("tile", "head"),
        P("tile", "head"),
        P("tile", "head"),
        P("tile", "head"),
        P("head"),
        P("head"),
        P("head"),
        P("head"),
        P(),
        P(),
        P(),
    )
    out_specs = P("tile", "head")
    small = mesh.shape["tile"] == TILES and mesh.shape["head"] == SHARDS
    return jax.shard_map(
        fused if small else per_device, mesh=mesh, in_specs=in_specs, out_specs=out_specs, check_vma=False
    )
```

profile of v0, /device:TPU:5, one launch (start us, length us, event | category | flops | bytes accessed | tf_op | source)
XLA Modules:
  0.0 36.2 jit_solution(13159230249304114354)
XLA Ops:
  0.0 0.0 copy-start.15
  0.0 0.7 %copy-done.15 = s32[8]{0:T(128)S(1)} copy-done((s32[8]{0:T(128)S(1)}, s32[8]{0:T(128)}, u32[]{:S(2)}) %copy-start.15) | copy-done | bytes 56
  0.7 0.7 %compare_reduce_fusion = (pred[]{:T(512)}, s32[]{:T(128)}) fusion(s32[8]{0:T(128)S(1)} %copy-done.15), kind=kLoop, calls=%fused_computation | loop fusion | flops 33 | bytes 45 | tf_op jit(solution)/shard_map/fused/reduce | solution.py:640
  1.4 0.0 copy-start.16
  1.4 0.0 copy-start.17
  1.4 0.7 %copy-done.16 = s32[8]{0:T(128)S(1)} copy-done((s32[8]{0:T(128)S(1)}, s32[8]{0:T(128)}, u32[]{:S(2)}) %copy-start.16) | copy-done | bytes 56
  2.0 0.0 copy-done.17
  2.6 32.9 %conditional.1 = (bf16[128,1280]{1,0:T(8,128)(2,1)S(1)}) conditional(s32[]{:T(128)} %clamp.3, (bf16[128,1280]{1,0:T(8,128)(2,1)}, bf16[128,1280]{1,0:T(8,128)(2,1)}, bf16[128,1280]{1,0:T(8,128)(2,1)}, bf16[128,1280]{1,0:T(8,128)(2,1)}, bf16[256,1280]{1,0:T(8,128)(2,1)}, /*index=5*/bf16[256,1280]{1,0:T(8,128)(2,1)}, ...), branch_computations={%region_1.2_spmd, %region_2.3_spmd, %region_3.4_spmd, %region_4.5_... | conditional | bytes 61532 | solution.py:641
  2.9 0.0 copy-start.14
  2.9 0.0 copy-start.9
  2.9 0.0 copy-start.4
  2.9 0.7 %copy-done.14 = f32[1280]{0:T(1024)S(1)} copy-done((f32[1280]{0:T(1024)S(1)}, f32[1280]{0:T(1024)}, u32[]{:S(2)}) %copy-start.14) | copy-done | bytes 5144 | tf_op jit(solution)/shard_map/cond
  3.6 0.0 copy-done.9
  3.6 0.0 copy-done.4
  3.6 31.6 %branch_4_fun.1 = bf16[128,1280]{1,0:T(8,128)(2,1)S(1)} custom-call(bf16[128,1280]{1,0:T(8,128)(2,1)} %get-tuple-element.221.q_in, bf16[128,1280]{1,0:T(8,128)(2,1)} %get-tuple-element.222.k_in, bf16[128,1280]{1,0:T(8,128)(2,1)} %get-tuple-element.223.v_in, bf16[128,1280]{1,0:T(8,128)(2,1)} %get-tuple-element.224.c_in, ...), custom_call_target="tpu_custom_call" | custom-call | tf_op jit(solution)/shard_map/cond/branch_4_fun/pallas_call | solution.py:641
  35.5 0.7 %copy.27 = bf16[128,1280]{1,0:T(8,128)(2,1)} copy(bf16[128,1280]{1,0:T(8,128)(2,1)S(1)} %get-tuple-element.238) | data formatting | bytes 655360
Async XLA Ops:
  0.0 0.7 %copy-start.15 = (s32[8]{0:T(128)S(1)}, s32[8]{0:T(128)}, u32[]{:S(2)}) copy-start(s32[8]{0:T(128)} %param.30) | copy-start | bytes 100
  1.4 0.7 %copy-start.16 = (s32[8]{0:T(128)S(1)}, s32[8]{0:T(128)}, u32[]{:S(2)}) copy-start(s32[8]{0:T(128)} %param.31) | copy-start | bytes 100
  1.4 0.7 %copy-start.17 = (s32[8]{0:T(128)S(1)}, s32[8]{0:T(128)}, u32[]{:S(2)}) copy-start(s32[8]{0:T(128)} %param.32) | copy-start | bytes 100
  2.9 0.7 %copy-start.14 = (f32[1280]{0:T(1024)S(1)}, f32[1280]{0:T(1024)}, u32[]{:S(2)}) copy-start(f32[1280]{0:T(1024)} %get-tuple-element.229.c_gain_in) | copy-start | bytes 15364 | tf_op jit(solution)/shard_map/cond
  2.9 0.7 %copy-start.9 = (f32[1280]{0:T(1024)S(1)}, f32[1280]{0:T(1024)}, u32[]{:S(2)}) copy-start(f32[1280]{0:T(1024)} %get-tuple-element.228.k_gain_in) | copy-start | bytes 15364 | tf_op jit(solution)/shard_map/cond
  2.9 0.7 %copy-start.4 = (f32[1280]{0:T(1024)S(1)}, f32[1280]{0:T(1024)}, u32[]{:S(2)}) copy-start(f32[1280]{0:T(1024)} %get-tuple-element.227.q_gain_in) | copy-start | bytes 15364 | tf_op jit(solution)/shard_map/cond
where the time goes:
time: 36.5 us; the launch traced here: 36.2 us
  Pallas kernels  31.6 us (87%)
  local copies, waits for them, and re-layouts  2.76 us (8%)
  other arithmetic  0.72 us (2%)
  between operations  0.58 us (2%)
  loops' own time  0.55 us (2%)
    pallas_call x1, Pallas kernels, fused(): lax.switch(start, [call(s) for s in range(TILES - SPAN + 1)], *operands)  31.6 us
    unnamed x7, local copies, waits for them, and re-layouts  2.05 us

commit v1 on v0

--- a/solution.py
+++ b/solution.py
@@ -233,12 +233,11 @@
     start,
     q_in, k_in, v_in, c_in, tk_in, tv_in,
     q_gain_in, k_gain_in, c_gain_in, t_gain_in,
-    cos_in, sin_in, item_in, count_in, len_in,
+    cos_in, sin_in, tile_item, row_count, text_len,
     out_ref,
     q_gain, k_gain, c_gain, t_gain,
-    cos_ref, sin_ref, tile_item, row_count, text_len,
-    q_raw, k_raw, c_raw, t_raw, t_val,
-    queries, cross, texts, text_out,
+    cos_ref, sin_ref,
+    raw, t_val, scales, queries, text_out,
     kbuf, vbuf, sums, live, text_live,
     in_sem, y_send, y_recv, z_send, z_recv, send_sem, recv_sem,
 ):
@@ -260,8 +259,9 @@
     loads = [
         pltpu.make_async_copy(src, dst, in_sem.at[i])
         for i, (src, dst) in enumerate(
-            ((k_in, k_raw), (q_in, q_raw), (c_in, c_raw), (tk_in, t_raw), (tv_in, t_val),
-             (item_in, tile_item), (count_in, row_count), (len_in, text_len), (cos_in, cos_ref), (sin_in, sin_ref),
+            ((k_in, raw.at[0:rows]), (q_in, raw.at[rows : 2 * rows]), (c_in, raw.at[2 * rows : 3 * rows]),
+             (tk_in, raw.at[3 * rows :]), (tv_in, t_val),
+             (cos_in, cos_ref), (sin_in, sin_ref),
              (k_gain_in, k_gain), (q_gain_in, q_gain), (c_gain_in, c_gain), (t_gain_in, t_gain))
         )
     ]
@@ -281,7 +281,7 @@
 
     near, far = plan_of(start, False), plan_of(start, True)
     split = start in (0, TILES - SPAN)
-    order = ([groups - 1] if split else []) + list(range(groups - 1 if split else groups))
+    shift = groups - 1 if split else 0
     base = pick(window(start))
 
     def plan(g):
@@ -297,15 +297,18 @@
             device_id_type=pl.DeviceIdType.MESH,
         )
 
-    def each_first(first, act):
-        for lane in range(max(len(f) for f in first)):
-            dests = [f[lane] if lane < len(f) else -1 for f in first]
-            dest = pick(dests)
+    def each_first(g, act):
+        firsts = [f[0] for f in ((near, far) if split else (near,))]
+        for lane in range(max(len(f) for first in firsts for f in first)):
+            lists = [[f[lane] if lane < len(f) else -1 for f in first] for first in firsts]
+            dest = pick(lists[0])
+            if lists[-1] != lists[0]:
+                dest = jnp.where(g == groups - 1, pick(lists[-1]), dest)
 
             def run(lane=lane, dest=dest):
                 act(lane, dest)
 
-            if -1 in dests:
+            if any(-1 in one for one in lists):
                 pl.when(dest >= 0)(run)
             else:
                 run()
@@ -351,7 +354,7 @@
         def of_first(lane, dest):
             send(buf.at[me, g], buf, kind, me, g, lane, dest).wait_send()
 
-        each_first(which[0], of_first)
+        each_first(g, of_first)
 
         def of_round(block, dests):
             for lane, dest in enumerate(dests):
@@ -363,13 +366,19 @@
 
         each_round(which[1], of_round)
 
-    for g in order:
-        own[g].wait()
-
-        def of_value(lane, dest, g=g):
+    for load in own:
+        load.wait()
+
+    def give_value(i, carry):
+        g = lax.rem(i + shift, groups)
+
+        def of_value(lane, dest):
             send(vbuf.at[me, g], vbuf, 0, me, g, lane, dest).start()
 
-        each_first(plan(g)[0], of_value)
+        each_first(g, of_value)
+        return carry
+
+    lax.fori_loop(0, groups, give_value, 0)
 
     for which, g0, g1 in ((near, 0, groups - 1 if split else groups), (far, groups - 1, groups)):
         if g1 == groups and which is far and not split:
@@ -383,13 +392,14 @@
                     for g in range(g0, g1):
                         vbuf[base + j, g] = jnp.zeros((rows, WIDE), jnp.bfloat16)
 
-    def partial(ref, r0):
+    def partial(i):
+        span = pl.ds(pl.multiple_of(i * rows, rows), rows)
         total = jnp.zeros((rows, HD), jnp.float32)
-        for i in range(heads):
-            part = ref[r0 : r0 + rows, i * HD : (i + 1) * HD].astype(jnp.float32)
+        for c in range(heads):
+            part = raw[span, c * HD : (c + 1) * HD].astype(jnp.float32)
             total = total + part * part
         column = jnp.sum(total, axis=1, keepdims=True)
-        return jnp.broadcast_to(column, (rows, HD)).T[0:8, :]
+        sums[shard, :, span] = jnp.broadcast_to(column, (rows, HD)).T[0:8, :]
 
     def share(o, slot, first):
         span = pl.ds(0, rows) if first else pl.ds(rows, 2 * rows + txt)
@@ -406,14 +416,19 @@
         for o in range(1, SHARDS):
             share(o, lax.rem(shard + o, SHARDS), first).wait_recv()
 
-    pieces = [(k_raw, 0), (q_raw, 0), (c_raw, 0)] + [(t_raw, r) for r in range(0, txt, rows)]
-    for i, (ref, r0) in enumerate(pieces):
-        if i < 4:
-            loads[i].wait()
-        sums[shard, :, i * rows : (i + 1) * rows] = partial(ref, r0)
-        if i in (0, len(pieces) - 1):
-            for o in range(1, SHARDS):
-                share(o, shard, i == 0).start()
+    def other_sums(i, carry):
+        partial(i)
+        return carry
+
+    loads[0].wait()
+    partial(0)
+    for o in range(1, SHARDS):
+        share(o, shard, True).start()
+    for load in loads[1:4]:
+        load.wait()
+    lax.fori_loop(1, 3 + txt // rows, other_sums, 0)
+    for o in range(1, SHARDS):
+        share(o, shard, False).start()
 
     for load in loads[5:]:
         load.wait()
@@ -435,12 +450,14 @@
 
     gather(True)
 
-    def scale_of(i):
-        span = slice(i * rows, (i + 1) * rows)
+    def set_scale(i, carry):
+        span = pl.ds(pl.multiple_of(i * rows, rows), rows)
         total = (sums[0, :, span] + sums[1, :, span]) + (sums[2, :, span] + sums[3, :, span])
         scale = lax.rsqrt(total / D + EPSILON)
-        return jnp.broadcast_to(scale[0:1, :], (HD, rows)).T
-
+        scales[span, :] = jnp.broadcast_to(scale[0:1, :], (HD, rows)).T
+        return carry
+
+    set_scale(0, 0)
     cosine = cos_ref[0:rows, :]
     sine = sin_ref[0:rows, :]
     for j in range(1, SPAN):
@@ -452,55 +469,42 @@
         partner = jnp.where(even, pltpu.roll(values, HD - 1, 1), pltpu.roll(values, 1, 1))
         return values * cosine + partner * sine
 
-    k_scale = scale_of(0)
-    for g in order:
-        for i in range(per):
-            cols = slice(g * WIDE + i * HD, g * WIDE + (i + 1) * HD)
-            scaled = k_raw[:, cols].astype(jnp.float32) * k_scale * k_gain[cols][None, :]
-            kbuf[me, g, :, i * HD : (i + 1) * HD] = turned(scaled).astype(jnp.bfloat16)
-
-        def of_key(lane, dest, g=g):
+    def scaled(row, amount, head, gain):
+        at = pl.ds(pl.multiple_of(head * HD, HD), HD)
+        span = slice(row * rows, (row + amount) * rows)
+        return raw[span, at].astype(jnp.float32) * scales[span, :] * gain[at][None, :]
+
+    def give_key(i, carry):
+        g = lax.rem(i + shift, groups)
+        for p in range(per):
+            kbuf[me, g, :, p * HD : (p + 1) * HD] = turned(scaled(0, 1, g * per + p, k_gain)).astype(jnp.bfloat16)
+
+        def of_key(lane, dest):
             send(kbuf.at[me, g], kbuf, 1, me, g, lane, dest).start()
 
-        each_first(plan(g)[0], of_key)
-
-    due = [(groups - 1, far[1][:2])] if split else []
-    due += [(g, near[1]) for g in range(groups - 1 if split else groups)]
-    due += [(groups - 1, far[1][2:])] if split else []
-
-    def pass_values(count):
-        for g, rounds in due[:count]:
-            pass_on(rounds, vbuf, 0, g)
-        del due[:count]
-
-    pass_values(1)
+        each_first(g, of_key)
+        return carry
+
+    lax.fori_loop(0, groups, give_key, 0)
+
+    if split:
+        pass_on(far[1][:2], vbuf, 0, groups - 1)
     gather(False)
-    q_scale = scale_of(1)
-    for i in range(heads):
-        cols = slice(i * HD, (i + 1) * HD)
-        scaled = q_raw[:, cols].astype(jnp.float32) * q_scale * q_gain[cols][None, :]
-        queries[i // per, :, (i % per) * HD : (i % per + 1) * HD] = turned(scaled).astype(jnp.bfloat16)
-    c_scale = scale_of(2)
-    for i in range(heads):
-        cols = slice(i * HD, (i + 1) * HD)
-        cross[i // per, :, (i % per) * HD : (i % per + 1) * HD] = (
-            c_raw[:, cols].astype(jnp.float32) * c_scale * c_gain[cols][None, :]
-        ).astype(jnp.bfloat16)
-    for r in range(txt // rows):
-        t_scale = scale_of(3 + r)
-        span = slice(r * rows, (r + 1) * rows)
-        for i in range(heads):
-            cols = slice(i * HD, (i + 1) * HD)
-            texts[i // per, span, (i % per) * HD : (i % per + 1) * HD] = (
-                t_raw[span, cols].astype(jnp.float32) * t_scale * t_gain[cols][None, :]
-            ).astype(jnp.bfloat16)
-
-    scale = 1.0 / math.sqrt(HD)
+    lax.fori_loop(1, 3 + txt // rows, set_scale, 0)
+
+    def set_query(g, carry):
+        for p in range(per):
+            queries[g, :, p * HD : (p + 1) * HD] = turned(scaled(1, 1, g * per + p, q_gain)).astype(jnp.bfloat16)
+        return carry
+
+    lax.fori_loop(0, groups, set_query, 0)
+
+    scale = math.log2(math.e) / math.sqrt(HD)
 
     def weigh(scores, dead):
         scores = jnp.where(dead > 0.5, BIG, scores * scale)
         highest = jnp.max(scores, axis=1, keepdims=True)
-        weights = jnp.exp(scores - highest)
+        weights = jnp.exp2(scores - highest)
         total = jnp.sum(weights, axis=1, keepdims=True)
         return weights.astype(jnp.bfloat16), total
 
@@ -509,18 +513,30 @@
 
     loads[4].wait()
 
-    pass_values(1)
-    dead_text = text_live[0:1, :]
-    for i in range(heads):
-        g, cols = i // per, slice((i % per) * HD, (i % per + 1) * HD)
-        weights, total = weigh(against(cross[g, :, cols], texts[g, :, cols]), dead_text)
-        mixed = jnp.dot(weights, t_val[:, i * HD : (i + 1) * HD], preferred_element_type=jnp.float32)
-        text_out[g, :, cols] = mixed / total
-        if i == heads // 2 - 1:
-            pass_values(2)
-    pass_values(len(due))
+    def text_group(g, carry):
+        dead = text_live[0:1, :]
+        for p in range(per):
+            cols = slice(p * HD, (p + 1) * HD)
+            head = g * per + p
+            query = scaled(2, 1, head, c_gain).astype(jnp.bfloat16)
+            words_here = scaled(3, txt // rows, head, t_gain).astype(jnp.bfloat16)
+            weights, total = weigh(against(query, words_here), dead)
+            at = pl.ds(pl.multiple_of(head * HD, HD), HD)
+            text_out[g, :, cols] = jnp.dot(weights, t_val[:, at], preferred_element_type=jnp.float32) / total
+        if split:
+
+            @pl.when(g < groups - 1)
+            def _():
+                pass_on(near[1], vbuf, 0, g)
+
+        else:
+            pass_on(near[1], vbuf, 0, g)
+        return carry
+
+    lax.fori_loop(0, groups, text_group, 0)
     if split:
         pass_on(far[1][:2], kbuf, 1, groups - 1)
+        pass_on(far[1][2:], vbuf, 0, groups - 1)
 
     def self_group(which, rounds, g):
         pass_on(rounds, kbuf, 1, g)
@@ -530,13 +546,10 @@
         for i in range(per):
             cols = slice(i * HD, (i + 1) * HD)
             query = queries[g, :, cols]
-            scores = jnp.concatenate([against(query, kbuf[base + j, g, :, cols]) for j in range(SPAN)], axis=1)
-            weights, total = weigh(scores, dead)
-            mixed = jnp.zeros((rows, HD), jnp.float32)
-            for j in range(SPAN):
-                mixed = mixed + jnp.dot(
-                    weights[:, j * rows : (j + 1) * rows], vbuf[base + j, g, :, cols], preferred_element_type=jnp.float32
-                )
+            keys = kbuf[pl.ds(base, SPAN), g, :, cols].reshape(SPAN * rows, HD)
+            values = vbuf[pl.ds(base, SPAN), g, :, cols].reshape(SPAN * rows, HD)
+            weights, total = weigh(against(query, keys), dead)
+            mixed = jnp.dot(weights, values, preferred_element_type=jnp.float32)
             at = pl.ds(pl.multiple_of(g * WIDE + i * HD, HD), HD)
             out_ref[:, at] = (mixed / total + text_out[g, :, cols]).astype(jnp.bfloat16)
 
@@ -591,34 +604,30 @@
     groups = width // WIDE
     cosine, sine = rotary_tables(rows)
     bf16, f32 = jnp.bfloat16, jnp.float32
-    hbm = pl.BlockSpec(memory_space=pl.ANY)
+    hbm = pl.BlockSpec(memory_space=pltpu.HBM)
     vmem = pl.BlockSpec(memory_space=pltpu.VMEM)
+    smem = pl.BlockSpec(memory_space=pltpu.SMEM)
 
     def call(start):
         return pl.pallas_call(
             functools.partial(kernel, start),
             out_shape=jax.ShapeDtypeStruct((rows, width), bf16),
-            in_specs=[hbm] * 15,
+            in_specs=[hbm] * 12 + [smem] * 3,
             out_specs=vmem,
             scratch_shapes=[pltpu.VMEM((width,), f32)] * 4
             + [pltpu.VMEM((SPAN * rows, HD), f32)] * 2
-            + [pltpu.SMEM((TILES,), jnp.int32)] * 3
             + [
-                pltpu.VMEM((rows, width), bf16),
-                pltpu.VMEM((rows, width), bf16),
-                pltpu.VMEM((rows, width), bf16),
+                pltpu.VMEM((3 * rows + txt, width), bf16),
                 pltpu.VMEM((txt, width), bf16),
-                pltpu.VMEM((txt, width), bf16),
+                pltpu.VMEM((3 * rows + txt, HD), f32),
                 pltpu.VMEM((groups, rows, WIDE), bf16),
-                pltpu.VMEM((groups, rows, WIDE), bf16),
-                pltpu.VMEM((groups, txt, WIDE), bf16),
                 pltpu.VMEM((groups, rows, WIDE), f32),
                 pltpu.VMEM((TILES, groups, rows, WIDE), bf16),
                 pltpu.VMEM((TILES, groups, rows, WIDE), bf16),
                 pltpu.VMEM((SHARDS, 8, 3 * rows + txt), f32),
                 pltpu.VMEM((8, SPAN * rows), f32),
                 pltpu.VMEM((8, txt), f32),
-                pltpu.SemaphoreType.DMA((14 + groups,)),
+                pltpu.SemaphoreType.DMA((11 + groups,)),
                 pltpu.SemaphoreType.DMA((SHARDS - 1,)),
                 pltpu.SemaphoreType.DMA((SHARDS,)),
                 pltpu.SemaphoreType.DMA((SHARDS - 1,)),

time: 36.5 us -> 36.1 us (0.989)
  the two profiles are of different devices: /device:TPU:5 before, /device:TPU:3 now
where the time goes in v1:
time: 36.1 us; the launch traced here: 35.8 us
  Pallas kernels  31.4 us (87%)
  local copies, waits for them, and re-layouts  2.76 us (8%)
  other arithmetic  0.72 us (2%)
  between operations  0.58 us (2%)
    pallas_call x1, Pallas kernels, fused(): lax.switch(start, [call(s) for s in range(TILES - SPAN + 1)], *operands)  31.4 us
    unnamed x7, local copies, waits for them, and re-layouts  2.05 us

profile of v1, /device:TPU:3, one launch (start us, length us, event | category | flops | bytes accessed | tf_op | source)
XLA Modules:
  0.0 35.8 jit_solution(1389830239096203196)
XLA Ops:
  0.0 0.0 copy-start.15
  0.0 0.7 %copy-done.15 = s32[8]{0:T(128)S(1)} copy-done((s32[8]{0:T(128)S(1)}, s32[8]{0:T(128)}, u32[]{:S(2)}) %copy-start.15) | copy-done | bytes 56
  0.7 0.7 %compare_reduce_fusion = (pred[]{:T(512)}, s32[]{:T(128)}) fusion(s32[8]{0:T(128)S(1)} %copy-done.15), kind=kLoop, calls=%fused_computation | loop fusion | flops 33 | bytes 45 | tf_op jit(solution)/shard_map/fused/reduce | solution.py:649
  1.4 0.0 copy-start.16
  1.4 0.0 copy-start.17
  1.4 0.7 %copy-done.16 = s32[8]{0:T(128)S(1)} copy-done((s32[8]{0:T(128)S(1)}, s32[8]{0:T(128)}, u32[]{:S(2)}) %copy-start.16) | copy-done | bytes 56
  2.0 0.0 copy-done.17
  2.6 32.4 %conditional.1 = (bf16[128,1280]{1,0:T(8,128)(2,1)S(1)}) conditional(s32[]{:T(128)} %clamp.3, (bf16[128,1280]{1,0:T(8,128)(2,1)}, bf16[128,1280]{1,0:T(8,128)(2,1)}, bf16[128,1280]{1,0:T(8,128)(2,1)}, bf16[128,1280]{1,0:T(8,128)(2,1)}, bf16[256,1280]{1,0:T(8,128)(2,1)}, /*index=5*/bf16[256,1280]{1,0:T(8,128)(2,1)}, ...), branch_computations={%region_1.2_spmd, %region_2.3_spmd, %region_3.4_spmd, %region_4.5_... | conditional | bytes 61532 | solution.py:650
  2.6 0.0 copy-start.11
  2.7 0.0 copy-start.6
  2.7 0.0 copy-start.1
  2.7 0.7 %copy-done.11 = f32[1280]{0:T(1024)S(1)} copy-done((f32[1280]{0:T(1024)S(1)}, f32[1280]{0:T(1024)}, u32[]{:S(2)}) %copy-start.11) | copy-done | bytes 5144 | tf_op jit(solution)/shard_map/cond
  3.3 0.0 copy-done.6
  3.4 0.0 copy-done.1
  3.4 31.4 %branch_1_fun.1 = bf16[128,1280]{1,0:T(8,128)(2,1)S(1)} custom-call(bf16[128,1280]{1,0:T(8,128)(2,1)} %get-tuple-element.176.q_in, bf16[128,1280]{1,0:T(8,128)(2,1)} %get-tuple-element.177.k_in, bf16[128,1280]{1,0:T(8,128)(2,1)} %get-tuple-element.178.v_in, bf16[128,1280]{1,0:T(8,128)(2,1)} %get-tuple-element.179.c_in, ...), custom_call_target="tpu_custom_call" | custom-call | tf_op jit(solution)/shard_map/cond/branch_1_fun/pallas_call | solution.py:650
  35.0 0.7 %copy.27 = bf16[128,1280]{1,0:T(8,128)(2,1)} copy(bf16[128,1280]{1,0:T(8,128)(2,1)S(1)} %get-tuple-element.238) | data formatting | bytes 655360
Async XLA Ops:
  0.0 0.7 %copy-start.15 = (s32[8]{0:T(128)S(1)}, s32[8]{0:T(128)}, u32[]{:S(2)}) copy-start(s32[8]{0:T(128)} %param.30) | copy-start | bytes 100
  1.4 0.7 %copy-start.16 = (s32[8]{0:T(128)S(1)}, s32[8]{0:T(128)}, u32[]{:S(2)}) copy-start(s32[8]{0:T(128)} %param.31) | copy-start | bytes 100
  1.4 0.7 %copy-start.17 = (s32[8]{0:T(128)S(1)}, s32[8]{0:T(128)}, u32[]{:S(2)}) copy-start(s32[8]{0:T(128)} %param.32) | copy-start | bytes 100
  2.6 0.7 %copy-start.11 = (f32[1280]{0:T(1024)S(1)}, f32[1280]{0:T(1024)}, u32[]{:S(2)}) copy-start(f32[1280]{0:T(1024)} %get-tuple-element.184.c_gain_in) | copy-start | bytes 15364 | tf_op jit(solution)/shard_map/cond
  2.7 0.7 %copy-start.6 = (f32[1280]{0:T(1024)S(1)}, f32[1280]{0:T(1024)}, u32[]{:S(2)}) copy-start(f32[1280]{0:T(1024)} %get-tuple-element.183.k_gain_in) | copy-start | bytes 15364 | tf_op jit(solution)/shard_map/cond
  2.7 0.7 %copy-start.1 = (f32[1280]{0:T(1024)S(1)}, f32[1280]{0:T(1024)}, u32[]{:S(2)}) copy-start(f32[1280]{0:T(1024)} %get-tuple-element.182.q_gain_in) | copy-start | bytes 15364 | tf_op jit(solution)/shard_map/cond

commit v2 on v1

--- a/solution.py
+++ b/solution.py
@@ -159,6 +159,7 @@
 SPAN = 4
 WIDE = 256
 BIG = -1e30
+LONG_WAY = False
 
 
 def needs(start):
@@ -280,7 +281,7 @@
     pl.semaphore_wait(barrier, TILES + SHARDS - 2)
 
     near, far = plan_of(start, False), plan_of(start, True)
-    split = start in (0, TILES - SPAN)
+    split = LONG_WAY and start in (0, TILES - SPAN)
     shift = groups - 1 if split else 0
     base = pick(window(start))
 
@@ -538,8 +539,7 @@
         pass_on(far[1][:2], kbuf, 1, groups - 1)
         pass_on(far[1][2:], vbuf, 0, groups - 1)
 
-    def self_group(which, rounds, g):
-        pass_on(rounds, kbuf, 1, g)
+    def self_group(which, g):
         arrive(which, vbuf, 0, g)
         arrive(which, kbuf, 1, g)
         dead = live[0:1, :]
@@ -553,18 +553,28 @@
             at = pl.ds(pl.multiple_of(g * WIDE + i * HD, HD), HD)
             out_ref[:, at] = (mixed / total + text_out[g, :, cols]).astype(jnp.bfloat16)
 
+    last = groups - 1 - split
+
     def near_group(g, carry):
-        self_group(near, near[1], g)
-        return carry
-
+        @pl.when(g < last)
+        def _():
+            pass_on(near[1], kbuf, 1, g + 1)
+
+        self_group(near, g)
+        return carry
+
+    pass_on(near[1], kbuf, 1, 0)
     def near_drain(g, carry):
         drain(near, vbuf, 0, g)
         drain(near, kbuf, 1, g)
         return carry
 
-    lax.fori_loop(0, groups - 1 if split else groups, near_group, 0)
+    lax.fori_loop(0, last, near_group, 0)
     if split:
-        self_group(far, far[1][2:], groups - 1)
+        pass_on(far[1][2:], kbuf, 1, groups - 1)
+    near_group(last, 0)
+    if split:
+        self_group(far, groups - 1)
         drain(far, vbuf, 0, groups - 1)
         drain(far, kbuf, 1, groups - 1)
     lax.fori_loop(0, groups - 1 if split else groups, near_drain, 0)

time: 36.1 us -> 31.3 us (0.87)
  the two profiles are of different devices: /device:TPU:3 before, /device:TPU:5 now
where the time goes in v2:
time: 31.3 us; the launch traced here: 30.8 us
  Pallas kernels  26.3 us (84%)
  local copies, waits for them, and re-layouts  2.76 us (9%)
  other arithmetic  0.72 us (2%)
  between operations  0.58 us (2%)
  loops' own time  0.47 us (2%)
    pallas_call x1, Pallas kernels, fused(): lax.switch(start, [call(s) for s in range(TILES - SPAN + 1)], *operands)  26.3 us
    unnamed x7, local copies, waits for them, and re-layouts  2.05 us
    another operation x1, other arithmetic, fused(): start = jnp.argmax(full).astype(jnp.int32)  0.72 us
    cond x6, local copies, waits for them, and re-layouts  0.71 us

profile of v2, /device:TPU:5, one launch (start us, length us, event | category | flops | bytes accessed | tf_op | source)
XLA Modules:
  0.0 30.8 jit_solution(3660880447271726984)
XLA Ops:
  0.0 0.0 copy-start.15
  0.0 0.7 %copy-done.15 = s32[8]{0:T(128)S(1)} copy-done((s32[8]{0:T(128)S(1)}, s32[8]{0:T(128)}, u32[]{:S(2)}) %copy-start.15) | copy-done | bytes 56
  0.7 0.7 %compare_reduce_fusion = (pred[]{:T(512)}, s32[]{:T(128)}) fusion(s32[8]{0:T(128)S(1)} %copy-done.15), kind=kLoop, calls=%fused_computation | loop fusion | flops 33 | bytes 45 | tf_op jit(solution)/shard_map/fused/reduce | solution.py:659
  1.4 0.0 copy-start.16
  1.4 0.0 copy-start.17
  1.4 0.7 %copy-done.16 = s32[8]{0:T(128)S(1)} copy-done((s32[8]{0:T(128)S(1)}, s32[8]{0:T(128)}, u32[]{:S(2)}) %copy-start.16) | copy-done | bytes 56
  2.0 0.0 copy-done.17
  2.6 27.4 %conditional.1 = (bf16[128,1280]{1,0:T(8,128)(2,1)S(1)}) conditional(s32[]{:T(128)} %clamp.3, (bf16[128,1280]{1,0:T(8,128)(2,1)}, bf16[128,1280]{1,0:T(8,128)(2,1)}, bf16[128,1280]{1,0:T(8,128)(2,1)}, bf16[128,1280]{1,0:T(8,128)(2,1)}, bf16[256,1280]{1,0:T(8,128)(2,1)}, /*index=5*/bf16[256,1280]{1,0:T(8,128)(2,1)}, ...), branch_computations={%region_1.2_spmd, %region_2.3_spmd, %region_3.4_spmd, %region_4.5_... | conditional | bytes 61532 | solution.py:660
  2.8 0.0 copy-start.14
  2.9 0.0 copy-start.9
  2.9 0.0 copy-start.4
  2.9 0.7 %copy-done.14 = f32[1280]{0:T(1024)S(1)} copy-done((f32[1280]{0:T(1024)S(1)}, f32[1280]{0:T(1024)}, u32[]{:S(2)}) %copy-start.14) | copy-done | bytes 5144 | tf_op jit(solution)/shard_map/cond
  3.5 0.0 copy-done.9
  3.6 0.0 copy-done.4
  3.6 26.3 %branch_4_fun.1 = bf16[128,1280]{1,0:T(8,128)(2,1)S(1)} custom-call(bf16[128,1280]{1,0:T(8,128)(2,1)} %get-tuple-element.221.q_in, bf16[128,1280]{1,0:T(8,128)(2,1)} %get-tuple-element.222.k_in, bf16[128,1280]{1,0:T(8,128)(2,1)} %get-tuple-element.223.v_in, bf16[128,1280]{1,0:T(8,128)(2,1)} %get-tuple-element.224.c_in, ...), custom_call_target="tpu_custom_call" | custom-call | tf_op jit(solution)/shard_map/cond/branch_4_fun/pallas_call | solution.py:660
  30.1 0.7 %copy.27 = bf16[128,1280]{1,0:T(8,128)(2,1)} copy(bf16[128,1280]{1,0:T(8,128)(2,1)S(1)} %get-tuple-element.238) | data formatting | bytes 655360
Async XLA Ops:
  0.0 0.7 %copy-start.15 = (s32[8]{0:T(128)S(1)}, s32[8]{0:T(128)}, u32[]{:S(2)}) copy-start(s32[8]{0:T(128)} %param.30) | copy-start | bytes 100
  1.4 0.7 %copy-start.16 = (s32[8]{0:T(128)S(1)}, s32[8]{0:T(128)}, u32[]{:S(2)}) copy-start(s32[8]{0:T(128)} %param.31) | copy-start | bytes 100
  1.4 0.7 %copy-start.17 = (s32[8]{0:T(128)S(1)}, s32[8]{0:T(128)}, u32[]{:S(2)}) copy-start(s32[8]{0:T(128)} %param.32) | copy-start | bytes 100
  2.8 0.7 %copy-start.14 = (f32[1280]{0:T(1024)S(1)}, f32[1280]{0:T(1024)}, u32[]{:S(2)}) copy-start(f32[1280]{0:T(1024)} %get-tuple-element.229.c_gain_in) | copy-start | bytes 15364 | tf_op jit(solution)/shard_map/cond
  2.9 0.7 %copy-start.9 = (f32[1280]{0:T(1024)S(1)}, f32[1280]{0:T(1024)}, u32[]{:S(2)}) copy-start(f32[1280]{0:T(1024)} %get-tuple-element.228.k_gain_in) | copy-start | bytes 15364 | tf_op jit(solution)/shard_map/cond
  2.9 0.7 %copy-start.4 = (f32[1280]{0:T(1024)S(1)}, f32[1280]{0:T(1024)}, u32[]{:S(2)}) copy-start(f32[1280]{0:T(1024)} %get-tuple-element.227.q_gain_in) | copy-start | bytes 15364 | tf_op jit(solution)/shard_map/cond
